TPU v7x, 32 devices: a whole 2x2x4 slice. The times are simulated.
32 devices in a mesh: rep: 2 (over x), tp: 8 (over z, y), sub: 2 (over core).
Axes of the slice: x: 2, y: 2, z: 4, core: 2. Of those that a mesh axis runs over, the one named last changes fastest.
Arguments:
- attn_out: bfloat16 [16, 2, 3, 2048], P('rep', 'sub', None, 'tp'), parts along dimension 0, may hold values from -6 to 6
- w_out: bfloat16 [2048, 16384], P('tp'), may hold values from -0.125 to 0.125
- residual: bfloat16 [96, 16384], P(('rep', 'tp', 'sub')), parts along dimension 0, may hold values from -6 to 6
- norm_gain: float32 [16384], replicated, may hold values from 0.1 to 1.9
- w_query: bfloat16 [16384, 2048], P(None, ('tp', 'sub')), may hold values from -0.046875 to 0.046875
Outputs:
- hidden_out: bfloat16 [96, 16384], P(('rep', 'tp', 'sub')), parts along dimension 0
- query: bfloat16 [96, 2048], P('rep', ('tp', 'sub')), parts along dimension 0
There are 2 independent parts, one for each index of `rep`. A program takes and returns all parts, laid end to end along the dimension named above; an argument that names none is the same for every part. Nothing has to cross between parts.
All inputs are finite; a program needn't handle non-finite values.
Results may differ from a plain program's by a relative error of at most 0.014.
Values may be sent and summed in bfloat16 or wider, within the bound.
A program may use at most 128 MiB of HBM per device.

v0:
```python
import jax
import jax.numpy as jnp
from jax import lax
from jax.sharding import PartitionSpec as P

HEAD = 128
BLOCK = 128


def rotation_table(size):
    index = jnp.arange(size, dtype=jnp.int32)
    common = index[:, None] & index[None, :]
    parity = jnp.zeros((size, size), jnp.int32)
    for shift_bit in range(size.bit_length() - 1):
        parity = parity + (common >> shift_bit & 1)
    signs = (1 - 2 * (parity % 2)).astype(jnp.float32)
    return signs / jnp.sqrt(jnp.float32(size))


def rotate(values, rotation):
    blocks = values.reshape(values.shape[0], -1, BLOCK)
    turned = jnp.einsum("tbi,ij->tbj", blocks, rotation, precision=lax.Precision.HIGHEST)
    return turned.reshape(values.shape)


def block_scales(values):
    blocks = values.reshape(values.shape[0], -1, BLOCK)
    return (jnp.max(jnp.abs(blocks), axis=-1) + 1e-06).astype(jnp.bfloat16)


def to_levels(values, scales):
    blocks = values.reshape(values.shape[0], -1, BLOCK)
    levels = (blocks / scales.astype(jnp.float32)[..., None]).astype(jnp.bfloat16)
    return lax.optimization_barrier(levels)


def from_levels(levels, scales):
    return (levels.astype(jnp.float32) * scales.astype(jnp.float32)[..., None]).reshape(
        levels.shape[0], -1
    )


def shards(attn_out, w_out, residual, norm_gain, w_query):
    rotation = rotation_table(BLOCK)
    across = lax.axis_size("tp")
    tok_local = residual.shape[0]
    width = w_out.shape[1]
    heads_here = w_out.shape[0] // HEAD
    my_rows = attn_out.reshape(across * tok_local, heads_here * HEAD)
    total = jnp.zeros((tok_local * lax.axis_size("tp"), width), jnp.float32)
    for head in range(heads_here):
        columns = my_rows[:, head * HEAD : (head + 1) * HEAD]
        weights = w_out[head * HEAD : (head + 1) * HEAD, :]
        partial_value = rotate(
            jnp.dot(columns, weights, preferred_element_type=jnp.float32), rotation
        )
        scales = block_scales(partial_value)
        levels, scales = (to_levels(partial_value, scales), scales)
        total = total + from_levels(levels, scales)
    summed = lax.psum_scatter(total, "tp", scatter_dimension=0, tiled=True)
    stream = residual.astype(jnp.float32) + rotate(summed, rotation)
    hidden_out = stream.astype(jnp.bfloat16)
    normed = (
        stream * lax.rsqrt(jnp.mean(stream * stream, axis=-1, keepdims=True) + 1e-05) * norm_gain
    )
    nscale = block_scales(normed)
    nlevel = to_levels(normed, nscale)
    restored = from_levels(
        lax.all_gather(nlevel, ("tp", "sub"), axis=0, tiled=True),
        lax.all_gather(nscale, ("tp", "sub"), axis=0, tiled=True),
    ).astype(jnp.bfloat16)
    product = jnp.dot(restored, w_query, preferred_element_type=jnp.float32)
    query = product.astype(jnp.bfloat16)
    return (hidden_out, query)


def solution(mesh):
    placed = (
        P("rep", "sub", None, "tp"),
        P("tp", None),
        P(("rep", "tp", "sub"), None),
        P(),
        P(None, ("tp", "sub")),
    )
    return jax.shard_map(
        shards,
        mesh=mesh,
        in_specs=placed,
        out_specs=(P(("rep", "tp", "sub"), None), P("rep", ("tp", "sub"))),
        check_vma=False,
    )
```

profile of v0, /device:TPU:0, one launch (start us, length us, event | category | flops | bytes accessed | tf_op | source)
XLA Modules:
  0.0 168.7 jit_solution(13887084672819180843)
XLA Ops:
  7.2 0.0 all-reduce.3.cloned.1.call-start
  7.2 0.7 copy.13
  7.9 2.9 %fusion.10 = f32[3,8,128,128]{3,1,2,0:T(8,128)S(1)} fusion(bf16[256,16384]{1,0:T(8,128)(2,1)} %param.6, bf16[24,256]{1,0:T(8,128)(2,1)S(1)} %reshape.53), kind=kOutput, calls=%fused_computation.15 | convolution fusion | flops 100663296 | bytes 5773312 | tf_op jit(solution)/shard_map/dot_general | solution.py:55
  10.8 2.9 %fusion.7 = f32[3,8,128,128]{3,1,2,0:T(8,128)S(1)} fusion(bf16[256,16384]{1,0:T(8,128)(2,1)} %param.6, bf16[24,256]{1,0:T(8,128)(2,1)S(1)} %reshape.53), kind=kOutput, calls=%fused_computation.14 | convolution fusion | flops 100663296 | bytes 5773312 | tf_op jit(solution)/shard_map/dot_general | solution.py:55
  13.7 0.3 copy.22
  13.9 1.6 abs_reduce_fusion
  15.6 0.3 copy.21
  15.9 1.6 abs_reduce_fusion.1
  17.5 0.2 divide_convert_fusion.1
  17.7 0.2 divide_convert_fusion
  18.0 0.4 multiply_add_fusion
  18.3 0.5 copy.16
  18.8 2.1 %copy.48 = f32[3,8,128,128]{3,1,2,0:T(8,128)} copy(f32[3,8,128,128]{3,2,1,0:T(8,128)S(1)} %bitcast.62) | data formatting | bytes 3145728
  20.9 0.0 copy-start.2
  20.9 0.0 copy-start
  20.9 0.0 copy-start.1
  20.9 0.0 all-reduce.3.cloned.1.call-update
  20.9 0.0 all-gather.3.cloned.1.call-start
  20.9 0.6 copy-done.2
  21.5 0.6 dynamic-slice
  22.7 89.9 %all-reduce.3.cloned.1.call-done = f32[24,16384]{1,0:T(8,128)} async-done(((f32[24,16384]{1,0:T(8,128)}), f32[24,16384]{1,0:T(8,128)}) %all-reduce.3.cloned.1.call-update) | async-done | bytes 1572880
  112.6 1.3 dynamic-slice_bitcast_fusion
  113.9 0.4 convolution_bitcast_fusion
  114.3 0.0 copy-done
  114.3 0.3 multiply_reduce_fusion
  114.6 0.0 copy-done.1
  114.6 0.9 multiply_bitcast_fusion
  115.5 0.1 fusion.16
  115.6 0.8 fusion.17
  116.4 0.0 all-gather.3.cloned.1.call-update
  116.4 19.6 %all-gather = bf16[16,3,128]{2,1,0:T(4,128)(2,1)S(1)} all-gather(bf16[1,3,128]{2,1,0:T(4,128)(2,1)S(1)} %get-tuple-element.4), channel_id=1, replica_groups=mesh['rep'=2,'tp'=8,'sub'=2] {'tp','sub'}, dimensions={0}, use_global_device_ids=true | all-gather | bytes 13056 | tf_op jit(solution)/shard_map/all_gather | solution.py:70
  136.0 19.6 %all-gather.3.cloned.1.call-done = bf16[48,128,128]{2,1,0:T(8,128)(2,1)} async-done(((bf16[3,128,128]{2,1,0:T(8,128)(2,1)}), bf16[48,128,128]{2,1,0:T(8,128)(2,1)}) %all-gather.3.cloned.1.call-update) | async-done | bytes 1572880 | tf_op jit(solution)/shard_map/all_gather | solution.py:69
  155.6 2.1 %multiply_convert_fusion = bf16[48,128,128]{2,1,0:T(8,128)(2,1)S(1)} fusion(bf16[48,128,128]{2,1,0:T(8,128)(2,1)} %all-gather.3.cloned.1.call-done, f32[48,128]{1,0:T(8,128)S(1)} %reshape.61), kind=kLoop, calls=%fused_computation.4 | loop fusion | flops 2359296 | bytes 3170304 | tf_op jit(solution)/shard_map/convert_element_type | solution.py:71
  157.7 4.1 %fusion.13 = bf16[48,128]{1,0:T(8,128)(2,1)} fusion(bf16[16384,128]{1,0:T(8,128)(2,1)} %param.9, bf16[6,8,128,128]{3,2,1,0:T(8,128)(2,1)S(1)} %bitcast.63), kind=kOutput, calls=%fused_computation.17 | convolution fusion | flops 201332736 | bytes 5779456 | tf_op jit(solution)/shard_map/dot_general | solution.py:72
  (5 shorter events, 0.1 us)
Async XLA Ops:
  7.2 105.5 %all-reduce.3.cloned.1.call-start = ((), (), s32[]{:S(2)}) async-start(), calls=%async_computation.1 | async-start | bytes 3145728
  20.9 0.7 copy-start.2
  20.9 93.5 %copy-start = (bf16[3,16384]{1,0:T(4,128)(2,1)S(1)}, bf16[3,16384]{1,0:T(4,128)(2,1)}, u32[]{:S(2)}) copy-start(bf16[3,16384]{1,0:T(4,128)(2,1)} %param.7) | copy-start | bytes 294916
  20.9 93.7 %copy-start.1 = (f32[16384]{0:T(1024)S(1)}, f32[16384]{0:T(1024)}, u32[]{:S(2)}) copy-start(f32[16384]{0:T(1024)} %param.8) | copy-start | bytes 196612
  20.9 134.8 %all-gather.3.cloned.1.call-start = ((), (), s32[]{:S(2)}) async-start(), calls=%async_computation | async-start | bytes 1671168 | tf_op jit(solution)/shard_map/all_gather | solution.py:69
Sparse Core Ops, SparseCore 0:
  21.0 91.5 all-reduce.2
  116.5 39.0 all-gather.2
where the time goes:
time: 169 us
  waiting for transfers between devices  110 us (65%)
  blocking collectives  19.6 us (12%)
  between operations  14.8 us (9%)
  matrix products  13.5 us (8%)
  local copies, waits for them, and re-layouts  6.27 us (4%)
  other arithmetic  4.91 us (3%)
    unnamed x3, waiting for transfers between devices  89.9 us
    all_gather x1, blocking collectives, shards(): lax.all_gather(nscale, ('tp', 'sub'), axis=0, tiled=True)  19.6 us
    all_gather x1, waiting for transfers between devices, shards(): lax.all_gather(nlevel, ('tp', 'sub'), axis=0, tiled=True)  19.6 us
    unnamed x12, local copies, waits for them, and re-layouts  5.76 us
    dot_general x2, matrix products, shards(): jnp.dot(columns, weights, preferred_element_type=jnp.float32)  5.71 us
    dot_general x1, matrix products, shards(): product = jnp.dot(restored, w_query, preferred_element_type=jnp.float32)  4.07 us
    dot_general x3, matrix products, rotate(): jnp.einsum('tbi,ij->tbj', blocks, rotation, precision=lax.Precision.HIGHEST)  3.68 us
  transfers between devices with their start and end apart: 2, of which 2 were waited for; matrix products, arithmetic and copies ran while one was open for 0% of the time, Pallas kernels for 0%

commit v1 on v0

v1 whole, which is shorter than its diff:
```python
import functools

import jax
import jax.numpy as jnp
from jax import lax
from jax.experimental import pallas as pl
from jax.experimental.pallas import tpu as pltpu
from jax.sharding import PartitionSpec as P

EPS = 1e-05
LANES = 128
MESH = pl.DeviceIdType.MESH


def kernel(
    outer,
    inner,
    fold,
    a_ref,
    res_ref,
    gain_ref,
    w_hbm,
    wq_hbm,
    hid_ref,
    q_ref,
    w_buf,
    wq_buf,
    part,
    recv1,
    mid,
    recv2,
    gath,
    acc,
    squares,
    w_sem,
    wq_sem,
    send1,
    got1,
    send2,
    got2,
    send_z,
    got_z,
    send_y,
    got_y,
    send_c,
    got_c,
):
    tp = outer * inner
    me = lax.axis_index("tp")
    sub = lax.axis_index("sub")
    zo, yi = me // inner, lax.rem(me, inner)
    toks, tok_local = a_ref.shape[0], res_ref.shape[0]
    cols = part.shape[2]
    width = cols * fold

    def chunk_of(z, y):
        return z * inner + y

    def z_peer(step):
        return lax.rem(zo + step, outer)

    def y_peer(step):
        return lax.rem(yi + step, inner)

    def columns(chunk, f):
        return pl.ds(pl.multiple_of(chunk * width + f * cols, LANES), cols)

    def peer_chunk(m):
        return z_peer(1 + m // (inner - 1)), y_peer(1 + lax.rem(m, inner - 1))

    def w_copy(chunk):
        where = pl.ds(pl.multiple_of(chunk * width, LANES), width)
        return pltpu.make_async_copy(w_hbm.at[:, where], w_buf.at[:, where], w_sem.at[chunk])

    def copy1(z, y):
        return pltpu.make_async_remote_copy(
            part.at[chunk_of(z, y)], recv1.at[yi, z], send1.at[chunk_of(z, y)], got1.at[yi, z],
            device_id={"tp": chunk_of(zo, y)}, device_id_type=MESH,
        )

    def arrive1(y, z):
        return pltpu.make_async_remote_copy(
            recv1.at[y, z], recv1.at[y, z], send1.at[0], got1.at[y, z],
            device_id={"tp": chunk_of(zo, y)}, device_id_type=MESH,
        )

    def copy2(z):
        return pltpu.make_async_remote_copy(
            mid.at[z], recv2.at[zo], send2.at[z], got2.at[zo],
            device_id={"tp": chunk_of(z, yi)}, device_id_type=MESH,
        )

    def arrive2(z):
        return pltpu.make_async_remote_copy(
            recv2.at[z], recv2.at[z], send2.at[0], got2.at[z],
            device_id={"tp": chunk_of(z, yi)}, device_id_type=MESH,
        )

    def spread_z(z):
        return pltpu.make_async_remote_copy(
            gath.at[sub, me], gath.at[sub, me], send_z.at[z], got_z.at[zo],
            device_id={"tp": chunk_of(z, yi)}, device_id_type=MESH,
        )

    def arrive_z(z):
        c = chunk_of(z, yi)
        return pltpu.make_async_remote_copy(
            gath.at[sub, c], gath.at[sub, c], send_z.at[0], got_z.at[z],
            device_id={"tp": c}, device_id_type=MESH,
        )

    def spread_y(z, y):
        c = chunk_of(z, yi)
        return pltpu.make_async_remote_copy(
            gath.at[sub, c], gath.at[sub, c], send_y.at[z, y], got_y.at[c],
            device_id={"tp": chunk_of(zo, y)}, device_id_type=MESH,
        )

    def arrive_y(z, y):
        c = chunk_of(z, y)
        return pltpu.make_async_remote_copy(
            gath.at[sub, c], gath.at[sub, c], send_y.at[0, 0], got_y.at[c],
            device_id={"tp": chunk_of(zo, y)}, device_id_type=MESH,
        )

    def spread_c(c):
        return pltpu.make_async_remote_copy(
            gath.at[sub, c], gath.at[sub, c], send_c.at[c], got_c.at[c],
            device_id={"sub": 1 - sub}, device_id_type=MESH,
        )

    def arrive_c(c):
        return pltpu.make_async_remote_copy(
            gath.at[1 - sub, c], gath.at[1 - sub, c], send_c.at[c], got_c.at[c],
            device_id={"sub": 1 - sub}, device_id_type=MESH,
        )

    def loop(count, body):
        if count <= 8:
            for step in range(count):
                body(step)
        else:
            lax.fori_loop(0, count, lambda i, _: (body(i), None)[1], None)

    peers1 = outer * (inner - 1)

    loop(peers1, lambda m: w_copy(chunk_of(*peer_chunk(m))).start())
    loop(outer, lambda k: w_copy(chunk_of(z_peer(1 + k), yi)).start())
    wq_copy = pltpu.make_async_copy(wq_hbm, wq_buf, wq_sem)
    wq_copy.start()
    barrier = pltpu.get_barrier_semaphore()

    def greet(**where):
        pl.semaphore_signal(barrier, inc=1, device_id=where, device_id_type=MESH)

    loop(outer - 1, lambda k: greet(tp=chunk_of(z_peer(1 + k), yi)))
    loop(inner - 1, lambda k: greet(tp=chunk_of(zo, y_peer(1 + k))))
    greet(sub=1 - sub)

    row = lax.broadcasted_iota(jnp.int32, (toks, cols), 0)

    def partial(chunk):
        w_copy(chunk).wait()
        pieces = []
        for f in range(fold):
            where = columns(chunk, f)
            piece = jnp.dot(a_ref[...], w_buf[:, where], preferred_element_type=jnp.float32)
            mine = res_ref[:, where].astype(jnp.float32)
            for r in range(tok_local):
                piece = piece + jnp.where(row == me * tok_local + r, mine[r : r + 1], 0.0)
            pieces.append(piece)
        return pieces[0] if fold == 1 else jnp.concatenate(pieces, axis=0)

    def first(m, wait_barrier=False):
        z, y = peer_chunk(m)
        part[chunk_of(z, y)] = partial(chunk_of(z, y)).astype(jnp.bfloat16)
        if wait_barrier:
            pl.semaphore_wait(barrier, outer + inner - 1)
        copy1(z, y).start()

    first(0, True)
    loop(peers1 - 1, lambda m: first(m + 1))

    def own(k):
        c = chunk_of(z_peer(1 + k), yi)
        part[c] = partial(c).astype(jnp.bfloat16)

    loop(outer, own)

    def reduced(z):
        total = part[chunk_of(z, yi)].astype(jnp.float32)
        for j in range(1, inner):
            y = y_peer(j)
            arrive1(y, z).wait_recv()
            total = total + recv1[y, z].astype(jnp.float32)
        return total

    def second(k):
        z = z_peer(1 + k)
        mid[z] = reduced(z).astype(jnp.bfloat16)
        copy2(z).start()

    loop(outer - 1, second)
    total = reduced(zo)
    for k in range(1, outer):
        z = z_peer(k)
        arrive2(z).wait_recv()
        total = total + recv2[z].astype(jnp.float32)
    gath[sub, me] = total.astype(jnp.bfloat16)

    loop(outer - 1, lambda k: spread_z(z_peer(1 + k)).start())
    acc[...] = jnp.zeros_like(acc)
    squares[...] = jnp.zeros_like(squares)

    def forward(k):
        z = z_peer(k)
        if not (isinstance(k, int) and k == 0):
            arrive_z(z).wait_recv()
        loop(inner - 1, lambda j: spread_y(z, y_peer(1 + j)).start())
        spread_c(chunk_of(z, yi)).start()

    def hand_over(k):
        z = z_peer(k)

        def one(j):
            y = y_peer(1 + j)
            arrive_y(z, y).wait_recv()
            spread_c(chunk_of(z, y)).start()

        loop(inner - 1, one)

    def use(chunk):
        arrive_c(chunk).wait_recv()
        both = [gath[s, chunk].astype(jnp.float32) for s in range(2)]
        own_rows = gath[sub, chunk].astype(jnp.float32)
        for f in range(fold):
            where = columns(chunk, f)
            span = slice(f * toks, (f + 1) * toks)
            x = jnp.concatenate([both[0][span], both[1][span]], axis=0)
            sq = x * x
            squares[...] += sum(sq[:, j * LANES : (j + 1) * LANES] for j in range(cols // LANES))
            y = (x * gain_ref[:, where]).astype(jnp.bfloat16)
            acc[...] += jnp.dot(y, wq_buf[where, :], preferred_element_type=jnp.float32)
            h = own_rows[span]
            for r in range(tok_local):
                hid_ref[r : r + 1, where] = jnp.sum(
                    jnp.where(row == me * tok_local + r, h, 0.0), axis=0, keepdims=True
                )

    def use_all(k):
        z = z_peer(k)
        loop(inner, lambda j: use(chunk_of(z, y_peer(j))))

    wq_copy.wait()
    forward(0)
    for k in range(1, outer + 2):
        if k < outer:
            forward(k)
        if 1 <= k <= outer:
            hand_over(k - 1)
        if k >= 2:
            use_all(k - 2)

    mean = jnp.sum(squares[...], axis=1, keepdims=True) / (width * tp)
    q_ref[...] = (acc[...] * lax.rsqrt(mean + EPS)).astype(q_ref.dtype)

    def done1(m):
        copy1(*peer_chunk(m)).wait_send()

    loop(peers1, done1)
    loop(outer - 1, lambda k: copy2(z_peer(1 + k)).wait_send())
    loop(outer - 1, lambda k: spread_z(z_peer(1 + k)).wait_send())
    loop(peers1, lambda m: spread_y(peer_chunk(m)[0], peer_chunk(m)[1]).wait_send())
    loop(tp, lambda c: spread_c(c).wait_send())


def shards(attn_out, w_out, residual, norm_gain, w_query):
    tp = lax.axis_size("tp")
    inner = 1
    while (2 * inner) ** 2 <= tp:
        inner *= 2
    outer = tp // inner
    tok_local = residual.shape[0]
    toks = tp * tok_local
    depth, width = w_out.shape
    heads = w_query.shape[1]
    fold = 1 if toks % 16 == 0 else 2
    rows, cols = toks * fold, width // tp // fold
    dma = pltpu.SemaphoreType.DMA
    bf16 = jnp.bfloat16
    vmem = pl.BlockSpec(memory_space=pltpu.VMEM)
    hidden, query = pl.pallas_call(
        functools.partial(kernel, outer, inner, fold),
        out_shape=(
            jax.ShapeDtypeStruct((tok_local, width), jnp.float32),
            jax.ShapeDtypeStruct((2 * toks, heads), jnp.float32),
        ),
        in_specs=[vmem] * 3 + [pl.BlockSpec(memory_space=pl.ANY)] * 2,
        out_specs=(vmem, vmem),
        scratch_shapes=[
            pltpu.VMEM((depth, width), bf16),
            pltpu.VMEM((width, heads), bf16),
            pltpu.VMEM((tp, rows, cols), bf16),
            pltpu.VMEM((inner, outer, rows, cols), bf16),
            pltpu.VMEM((outer, rows, cols), bf16),
            pltpu.VMEM((outer, rows, cols), bf16),
            pltpu.VMEM((2, tp, rows, cols), bf16),
            pltpu.VMEM((2 * toks, heads), jnp.float32),
            pltpu.VMEM((2 * toks, LANES), jnp.float32),
            dma((tp,)),
            dma,
            dma((tp,)),
            dma((inner, outer)),
            dma((outer,)),
            dma((outer,)),
            dma((outer,)),
            dma((outer,)),
            dma((outer, inner)),
            dma((tp,)),
            dma((tp,)),
            dma((tp,)),
        ],
        compiler_params=pltpu.CompilerParams(
            collective_id=0, has_side_effects=True, vmem_limit_bytes=58 * 2**20
        ),
        cost_estimate=pl.CostEstimate(
            flops=2 * toks * depth * width + 4 * toks * width * heads,
            bytes_accessed=2 * (depth + heads) * width,
            transcendentals=0,
        ),
    )(attn_out.reshape(toks, depth), residual, norm_gain.reshape(1, width), w_out, w_query)
    query = query.reshape(2, tp, tok_local, heads).transpose(1, 0, 2, 3).reshape(2 * toks, heads)
    return hidden.astype(bf16), query.astype(bf16)


def solution(mesh):
    placed = (
        P("rep", "sub", None, "tp"),
        P("tp", None),
        P(("rep", "tp", "sub"), None),
        P(),
        P(None, ("tp", "sub")),
    )
    return jax.shard_map(
        shards,
        mesh=mesh,
        in_specs=placed,
        out_specs=(P(("rep", "tp", "sub"), None), P("rep", ("tp", "sub"))),
        check_vma=False,
    )
```

time: 169 us -> 43.9 us (0.26)
  the two profiles are of different devices: /device:TPU:0 before, /device:TPU:11 now
where the time goes in v1:
time: 43.9 us; the launch traced here: 43.6 us
  Pallas kernels  38.6 us (88%)
  other arithmetic  2.39 us (5%)
  local copies, waits for them, and re-layouts  1.98 us (5%)
  between operations  0.65 us (1%)
    pallas_call x1, Pallas kernels, shards(): pl.pallas_call(functools.partial(kernel, outer, inner, fold), out_shape=(...  38.6 us
    convert_element_type x2, other arithmetic, shards(): return (hidden.astype(bf16), query.astype(bf16))  2.39 us

profile of v1, /device:TPU:11, one launch (start us, length us, event | category | flops | bytes accessed | tf_op | source)
XLA Modules:
  0.0 43.6 jit_solution(16528328814891487334)
XLA Ops:
  0.6 0.7 %copy.9 = bf16[8,1,3,256]{3,2,0,1:T(4,128)(2,1)S(1)} copy(bf16[8,1,3,256]{3,0,2,1:T(8,128)(2,1)} %param.5) | data formatting | bytes 24576 | tf_op args[0]
  1.3 0.6 %reshape.14.a_ref = bf16[24,256]{1,0:T(8,128)(2,1)} reshape(bf16[8,1,3,256]{3,2,0,1:T(4,128)(2,1)S(1)} %copy.9) | data formatting | bytes 24576 | tf_op jit(solution)/shard_map/reshape | solution.py:331
  2.0 38.6 %shard_map.68 = (f32[3,16384]{1,0:T(4,128)}, f32[48,128]{1,0:T(8,128)}) custom-call(bf16[24,256]{1,0:T(8,128)(2,1)} %reshape.14.a_ref, bf16[3,16384]{1,0:T(4,128)(2,1)} %res_ref.1, f32[1,16384]{1,0:T(1,128)} %bitcast.4, bf16[256,16384]{1,0:T(8,128)(2,1)} %w_hbm.1, bf16[16384,128]{1,0:T(8,128)(2,1)} %wq_hbm.1), custom_call_target="tpu_custom_call" | custom-call | flops 402653184 | bytes 12582912 | tf_op jit(solution)/shard_map/pallas_call | solution.py:292
  40.6 1.7 %convert_element_type.15 = bf16[3,16384]{1,0:T(4,128)(2,1)} convert(f32[3,16384]{1,0:T(4,128)} %get-tuple-element.4) | non-fusion elementwise | flops 49152 | bytes 294912 | tf_op jit(solution)/shard_map/convert_element_type | solution.py:333
  42.2 0.7 %convert_element_type.16 = bf16[48,128]{1,0:T(8,128)(2,1)S(1)} convert(f32[48,128]{1,0:T(8,128)} %get-tuple-element.5) | non-fusion elementwise | flops 6144 | bytes 36864 | tf_op jit(solution)/shard_map/convert_element_type | solution.py:333
  43.0 0.6 %convert_element_type.19 = bf16[48,128]{1,0:T(8,128)(2,1)} reshape(bf16[8,2,3,128]{3,2,1,0:T(4,128)(2,1)S(1)} %copy.10) | data formatting | bytes 24576 | tf_op jit(solution)/shard_map/convert_element_type | solution.py:333
  (2 shorter events, 0.0 us)

commit v2 on v1

v2 whole, which is shorter than its diff:
```python
import functools

import jax
import jax.numpy as jnp
from jax import lax
from jax.experimental import pallas as pl
from jax.experimental.pallas import tpu as pltpu
from jax.sharding import PartitionSpec as P

EPS = 1e-05
LANES = 128
SPLIT = 2
MESH = pl.DeviceIdType.MESH


def kernel(
    outer,
    inner,
    fold,
    split,
    a_ref,
    res_ref,
    gain_ref,
    w_hbm,
    wq_hbm,
    hid_ref,
    q_ref,
    w_buf,
    wq_buf,
    part,
    recv1,
    mid,
    recv2,
    gath,
    acc,
    squares,
    q_rows,
    w_sem,
    wq_sem,
    send1,
    got1,
    send2,
    got2,
    send_z,
    got_z,
    send_y,
    got_y,
    send_c,
    got_c,
):
    tp = outer * inner
    me = lax.axis_index("tp")
    sub = lax.axis_index("sub")
    zo, yi = me // inner, lax.rem(me, inner)
    tok_local = res_ref.shape[0]
    toks = tp * tok_local
    cols = part.shape[3]
    piece_width = cols * fold
    width = piece_width * split

    def chunk_of(z, y):
        return z * inner + y

    def z_peer(step):
        return lax.rem(zo + step, outer)

    def y_peer(step):
        return lax.rem(yi + step, inner)

    def columns(chunk, h, f):
        return pl.ds(pl.multiple_of(chunk * width + h * piece_width + f * cols, LANES), cols)

    def peer_chunk(m):
        return z_peer(1 + m // (inner - 1)), y_peer(1 + lax.rem(m, inner - 1))

    def w_copy(chunk, h):
        where = pl.ds(pl.multiple_of(chunk * width + h * piece_width, LANES), piece_width)
        return pltpu.make_async_copy(w_hbm.at[:, where], w_buf.at[:, where], w_sem.at[chunk, h])

    def remote(src, dst, send, got, **where):
        return pltpu.make_async_remote_copy(
            src, dst, send, got, device_id=where, device_id_type=MESH
        )

    def copy1(z, y, h):
        c = chunk_of(z, y)
        return remote(
            part.at[c, h], recv1.at[yi, z, h], send1.at[c, h], got1.at[yi, z, h], tp=chunk_of(zo, y)
        )

    def arrive1(y, z, h):
        slot = recv1.at[y, z, h]
        return remote(slot, slot, send1.at[0, 0], got1.at[y, z, h], tp=chunk_of(zo, y))

    def copy2(z, h):
        return remote(
            mid.at[z, h], recv2.at[zo, h], send2.at[z, h], got2.at[zo, h], tp=chunk_of(z, yi)
        )

    def arrive2(z, h):
        slot = recv2.at[z, h]
        return remote(slot, slot, send2.at[0, 0], got2.at[z, h], tp=chunk_of(z, yi))

    def spread_z(z, h):
        slot = gath.at[sub, me, h]
        return remote(slot, slot, send_z.at[z, h], got_z.at[zo, h], tp=chunk_of(z, yi))

    def arrive_z(z, h):
        c = chunk_of(z, yi)
        slot = gath.at[sub, c, h]
        return remote(slot, slot, send_z.at[0, 0], got_z.at[z, h], tp=c)

    def spread_y(z, y, h):
        c = chunk_of(z, yi)
        slot = gath.at[sub, c, h]
        return remote(slot, slot, send_y.at[z, y, h], got_y.at[c, h], tp=chunk_of(zo, y))

    def arrive_y(z, y, h):
        c = chunk_of(z, y)
        slot = gath.at[sub, c, h]
        return remote(slot, slot, send_y.at[0, 0, 0], got_y.at[c, h], tp=chunk_of(zo, y))

    def spread_c(c, h):
        slot = gath.at[sub, c, h]
        return remote(slot, slot, send_c.at[c, h], got_c.at[c, h], sub=1 - sub)

    def arrive_c(c, h):
        slot = gath.at[1 - sub, c, h]
        return remote(slot, slot, send_c.at[c, h], got_c.at[c, h], sub=1 - sub)

    def loop(count, body):
        if count <= 8:
            for step in range(count):
                body(step)
        else:
            lax.fori_loop(0, count, lambda i, _: (body(i), None)[1], None)

    peers1 = outer * (inner - 1)

    for h in range(split):
        loop(peers1, lambda m: w_copy(chunk_of(*peer_chunk(m)), h).start())
    for h in range(split):
        loop(outer, lambda k: w_copy(chunk_of(z_peer(1 + k), yi), h).start())
    wq_copy = pltpu.make_async_copy(wq_hbm, wq_buf, wq_sem)
    wq_copy.start()
    barrier = pltpu.get_barrier_semaphore()

    def greet(**where):
        pl.semaphore_signal(barrier, inc=1, device_id=where, device_id_type=MESH)

    loop(outer - 1, lambda k: greet(tp=chunk_of(z_peer(1 + k), yi)))
    loop(inner - 1, lambda k: greet(tp=chunk_of(zo, y_peer(1 + k))))
    greet(sub=1 - sub)

    row = lax.broadcasted_iota(jnp.int32, (toks, cols), 0)

    def partial(chunk, h):
        w_copy(chunk, h).wait()
        pieces = []
        for f in range(fold):
            where = columns(chunk, h, f)
            piece = jnp.dot(a_ref[...], w_buf[:, where], preferred_element_type=jnp.float32)
            mine = res_ref[:, where].astype(jnp.float32)
            for r in range(tok_local):
                piece = piece + jnp.where(row == r * tp + me, mine[r : r + 1], 0.0)
            pieces.append(piece)
        return pieces[0] if fold == 1 else jnp.concatenate(pieces, axis=0)

    def first(m, h, wait_barrier=False):
        z, y = peer_chunk(m)
        part[chunk_of(z, y), h] = partial(chunk_of(z, y), h).astype(jnp.bfloat16)
        if wait_barrier:
            pl.semaphore_wait(barrier, outer + inner - 1)
        copy1(z, y, h).start()

    def reduced(z, h):
        total = partial(chunk_of(z, yi), h)
        for j in range(1, inner):
            y = y_peer(j)
            arrive1(y, z, h).wait_recv()
            total = total + recv1[y, z, h].astype(jnp.float32)
        return total

    def second(h):
        def one(k):
            z = z_peer(1 + k)
            mid[z, h] = reduced(z, h).astype(jnp.bfloat16)
            copy2(z, h).start()

        loop(outer - 1, one)

    def third(h):
        total = reduced(zo, h)
        for k in range(1, outer):
            z = z_peer(k)
            arrive2(z, h).wait_recv()
            total = total + recv2[z, h].astype(jnp.float32)
        gath[sub, me, h] = total.astype(jnp.bfloat16)
        loop(outer - 1, lambda k: spread_z(z_peer(1 + k), h).start())
        forward(0, h)

    def forward(k, h):
        z = z_peer(k)
        loop(inner - 1, lambda j: spread_y(z, y_peer(1 + j), h).start())
        spread_c(chunk_of(z, yi), h).start()

    def fourth(h):
        def one(k):
            arrive_z(z_peer(1 + k), h).wait_recv()
            forward(1 + k, h)

        loop(outer - 1, one)

    def fifth(h):
        def one(m):
            z, y = z_peer(m // (inner - 1)), y_peer(1 + lax.rem(m, inner - 1))
            arrive_y(z, y, h).wait_recv()
            spread_c(chunk_of(z, y), h).start()

        loop(peers1, one)

    def use(chunk, h):
        arrive_c(chunk, h).wait_recv()
        both = [gath[s, chunk, h].astype(jnp.float32) for s in range(2)]
        own_rows = gath[sub, chunk, h].astype(jnp.float32)
        for f in range(fold):
            where = columns(chunk, h, f)
            span = slice(f * toks, (f + 1) * toks)
            x = jnp.concatenate([both[0][span], both[1][span]], axis=0)
            sq = x * x
            squares[...] += sum(sq[:, j * LANES : (j + 1) * LANES] for j in range(cols // LANES))
            y = (x * gain_ref[:, where]).astype(jnp.bfloat16)
            acc[...] += jnp.dot(y, wq_buf[where, :], preferred_element_type=jnp.float32)
            h_rows = own_rows[span]
            mine = [
                jnp.sum(jnp.where(row == r * tp + me, h_rows, 0.0), axis=0, keepdims=True)
                for r in range(tok_local)
            ]
            hid_ref[:, where] = jnp.concatenate(mine, axis=0).astype(hid_ref.dtype)

    def sixth(h):
        def one(m):
            use(chunk_of(z_peer(m // inner), y_peer(lax.rem(m, inner))), h)

        loop(tp, one)

    first(0, 0, True)
    loop(peers1 - 1, lambda m: first(m + 1, 0))
    for h in range(1, split):
        loop(peers1, lambda m: first(m, h))
    acc[...] = jnp.zeros_like(acc)
    squares[...] = jnp.zeros_like(squares)
    stages = (second, third, fourth, fifth, sixth)
    for t in range(split + len(stages) - 1):
        if t == len(stages) - 1:
            wq_copy.wait()
        for n, stage in enumerate(stages):
            if 0 <= t - n < split:
                stage(t - n)

    mean = jnp.sum(squares[...], axis=1, keepdims=True) / (width * tp)
    q = acc[...] * lax.rsqrt(mean + EPS)
    for s in range(2):
        for r in range(tok_local):
            start = s * toks + r * tp
            q_rows[pl.ds(s * tok_local + r, tp, stride=2 * tok_local), :] = q[start : start + tp]
    q_ref[...] = q_rows[...].astype(q_ref.dtype)

    for h in range(split):
        loop(peers1, lambda m: copy1(*peer_chunk(m), h).wait_send())
        loop(outer - 1, lambda k: copy2(z_peer(1 + k), h).wait_send())
        loop(outer - 1, lambda k: spread_z(z_peer(1 + k), h).wait_send())
        loop(peers1, lambda m: spread_y(*peer_chunk(m), h).wait_send())
        loop(tp, lambda c: spread_c(c, h).wait_send())


def hand_out(hid_in, q_in, hid_out, q_out):
    hid_out[...] = hid_in[...]
    q_out[...] = q_in[...]


def shards(attn_out, w_out, residual, norm_gain, w_query):
    tp = lax.axis_size("tp")
    inner = 1
    while (2 * inner) ** 2 <= tp:
        inner *= 2
    outer = tp // inner
    tok_local = residual.shape[0]
    toks = tp * tok_local
    depth, width = w_out.shape
    heads = w_query.shape[1]
    fold = 1 if toks % 16 == 0 else 2
    split = max(1, min(SPLIT, width // tp // fold // LANES))
    rows, cols = toks * fold, width // tp // fold // split
    a = attn_out.transpose(1, 2, 0, 3).reshape(toks, depth)
    dma = pltpu.SemaphoreType.DMA
    bf16 = jnp.bfloat16
    vmem = pl.BlockSpec(memory_space=pltpu.VMEM)
    hbm = pl.BlockSpec(memory_space=pl.ANY)
    outs = (
        jax.ShapeDtypeStruct((tok_local, width), bf16),
        jax.ShapeDtypeStruct((2 * toks, heads), bf16),
    )
    results = pl.pallas_call(
        functools.partial(kernel, outer, inner, fold, split),
        out_shape=outs,
        in_specs=[vmem] * 3 + [hbm] * 2,
        out_specs=(vmem, vmem),
        scratch_shapes=[
            pltpu.VMEM((depth, width), bf16),
            pltpu.VMEM((width, heads), bf16),
            pltpu.VMEM((tp, split, rows, cols), bf16),
            pltpu.VMEM((inner, outer, split, rows, cols), bf16),
            pltpu.VMEM((outer, split, rows, cols), bf16),
            pltpu.VMEM((outer, split, rows, cols), bf16),
            pltpu.VMEM((2, tp, split, rows, cols), bf16),
            pltpu.VMEM((2 * toks, heads), jnp.float32),
            pltpu.VMEM((2 * toks, LANES), jnp.float32),
            pltpu.VMEM((2 * toks, heads), jnp.float32),
            dma((tp, split)),
            dma,
            dma((tp, split)),
            dma((inner, outer, split)),
            dma((outer, split)),
            dma((outer, split)),
            dma((outer, split)),
            dma((outer, split)),
            dma((outer, inner, split)),
            dma((tp, split)),
            dma((tp, split)),
            dma((tp, split)),
        ],
        compiler_params=pltpu.CompilerParams(
            collective_id=0, has_side_effects=True, vmem_limit_bytes=58 * 2**20
        ),
        cost_estimate=pl.CostEstimate(
            flops=2 * toks * depth * width + 4 * toks * width * heads,
            bytes_accessed=2 * (depth + heads) * width,
            transcendentals=0,
        ),
    )(a, residual, norm_gain.reshape(1, width), w_out, w_query)
    return pl.pallas_call(hand_out, out_shape=outs, in_specs=[vmem] * 2, out_specs=(vmem, vmem))(
        *results
    )


def solution(mesh):
    placed = (
        P("rep", "sub", None, "tp"),
        P("tp", None),
        P(("rep", "tp", "sub"), None),
        P(),
        P(None, ("tp", "sub")),
    )
    return jax.shard_map(
        shards,
        mesh=mesh,
        in_specs=placed,
        out_specs=(P(("rep", "tp", "sub"), None), P("rep", ("tp", "sub"))),
        check_vma=False,
    )
```

time: 43.9 us -> 38.5 us (0.88)
  the two profiles are of different devices: /device:TPU:11 before, /device:TPU:0 now
where the time goes in v2:
time: 38.5 us; the launch traced here: 38.1 us
  Pallas kernels  37.5 us (97%)
  between operations  0.64 us (2%)
    pallas_call x1, Pallas kernels, shards(): pl.pallas_call(functools.partial(kernel, outer, inner, fold, split), out_...  35.9 us
    pallas_call x1, Pallas kernels, shards(): pl.pallas_call(hand_out, out_shape=outs, in_specs=[vmem] * 2, out_specs=(...  1.58 us

profile of v2, /device:TPU:0, one launch (start us, length us, event | category | flops | bytes accessed | tf_op | source)
XLA Modules:
  0.0 38.1 jit_solution(15100622701946384611)
XLA Ops:
  0.6 35.9 %shard_map.68 = (bf16[3,16384]{1,0:T(4,128)(2,1)}, bf16[48,128]{1,0:T(8,128)(2,1)}) custom-call(bf16[24,256]{1,0:T(8,128)(2,1)} %bitcast.5, bf16[3,16384]{1,0:T(4,128)(2,1)} %res_ref.1, f32[1,16384]{1,0:T(1,128)} %bitcast.4, bf16[256,16384]{1,0:T(8,128)(2,1)} %w_hbm.1, bf16[16384,128]{1,0:T(8,128)(2,1)} %wq_hbm.1), custom_call_target="tpu_custom_call" | custom-call | flops 402653184 | bytes 12582912 | tf_op jit(solution)/shard_map/pallas_call | solution.py:304
  36.5 1.6 %shard_map.69 = (bf16[3,16384]{1,0:T(4,128)(2,1)}, bf16[48,128]{1,0:T(8,128)(2,1)}) custom-call(bf16[3,16384]{1,0:T(4,128)(2,1)} %get-tuple-element.4.hid_in, bf16[48,128]{1,0:T(8,128)(2,1)} %get-tuple-element.5.q_in), custom_call_target="tpu_custom_call" | custom-call | tf_op jit(solution)/shard_map/pallas_call | solution.py:342

commit v3 on v2

--- a/solution.py
+++ b/solution.py
@@ -64,6 +64,9 @@
     def z_peer(step):
         return lax.rem(zo + step, outer)
 
+    def z_source(step):
+        return lax.rem(zo + outer - step, outer)
+
     def y_peer(step):
         return lax.rem(yi + step, inner)
 
@@ -200,24 +203,16 @@
         forward(0, h)
 
     def forward(k, h):
-        z = z_peer(k)
+        z = z_source(k)
         loop(inner - 1, lambda j: spread_y(z, y_peer(1 + j), h).start())
         spread_c(chunk_of(z, yi), h).start()
 
     def fourth(h):
         def one(k):
-            arrive_z(z_peer(1 + k), h).wait_recv()
+            arrive_z(z_source(1 + k), h).wait_recv()
             forward(1 + k, h)
 
         loop(outer - 1, one)
-
-    def fifth(h):
-        def one(m):
-            z, y = z_peer(m // (inner - 1)), y_peer(1 + lax.rem(m, inner - 1))
-            arrive_y(z, y, h).wait_recv()
-            spread_c(chunk_of(z, y), h).start()
-
-        loop(peers1, one)
 
     def use(chunk, h):
         arrive_c(chunk, h).wait_recv()
@@ -238,11 +233,24 @@
             ]
             hid_ref[:, where] = jnp.concatenate(mine, axis=0).astype(hid_ref.dtype)
 
-    def sixth(h):
-        def one(m):
-            use(chunk_of(z_peer(m // inner), y_peer(lax.rem(m, inner))), h)
-
-        loop(tp, one)
+    def use_far(k, h):
+        loop(inner - 1, lambda j: use(chunk_of(z_source(k), y_peer(1 + j)), h))
+
+    def fifth(h):
+        def one(k):
+            z = z_source(k)
+
+            def hand_over(j):
+                y = y_peer(1 + j)
+                arrive_y(z, y, h).wait_recv()
+                spread_c(chunk_of(z, y), h).start()
+
+            if h > 0:
+                use_far(k, h - 1)
+            use(chunk_of(z, yi), h)
+            loop(inner - 1, hand_over)
+
+        loop(outer, one)
 
     first(0, 0, True)
     loop(peers1 - 1, lambda m: first(m + 1, 0))
@@ -250,13 +258,14 @@
         loop(peers1, lambda m: first(m, h))
     acc[...] = jnp.zeros_like(acc)
     squares[...] = jnp.zeros_like(squares)
-    stages = (second, third, fourth, fifth, sixth)
+    stages = (second, third, fourth, fifth)
     for t in range(split + len(stages) - 1):
         if t == len(stages) - 1:
             wq_copy.wait()
         for n, stage in enumerate(stages):
             if 0 <= t - n < split:
                 stage(t - n)
+    loop(outer, lambda k: use_far(k, split - 1))
 
     mean = jnp.sum(squares[...], axis=1, keepdims=True) / (width * tp)
     q = acc[...] * lax.rsqrt(mean + EPS)

time: 38.5 us -> 35.9 us (0.932)
  Pallas kernels: 37.5 us -> 34.9 us
    pallas_call x1, Pallas kernels: 35.9 us -> 33.4 us  [shards(): pl.pallas_call(functools.partial(kernel, outer, inner, fold, split), out_...]
where the time goes in v3:
time: 35.9 us; the launch traced here: 35.6 us
  Pallas kernels  34.9 us (97%)
  between operations  0.64 us (2%)
    pallas_call x1, Pallas kernels, shards(): pl.pallas_call(functools.partial(kernel, outer, inner, fold, split), out_...  33.4 us
    pallas_call x1, Pallas kernels, shards(): pl.pallas_call(hand_out, out_shape=outs, in_specs=[vmem] * 2, out_specs=(...  1.58 us

profile of v3, /device:TPU:0, one launch (start us, length us, event | category | flops | bytes accessed | tf_op | source)
XLA Modules:
  0.0 35.6 jit_solution(9842244731398317958)
XLA Ops:
  0.6 33.4 %shard_map.68 = (bf16[3,16384]{1,0:T(4,128)(2,1)}, bf16[48,128]{1,0:T(8,128)(2,1)}) custom-call(bf16[24,256]{1,0:T(8,128)(2,1)} %bitcast.5, bf16[3,16384]{1,0:T(4,128)(2,1)} %res_ref.1, f32[1,16384]{1,0:T(1,128)} %bitcast.4, bf16[256,16384]{1,0:T(8,128)(2,1)} %w_hbm.1, bf16[16384,128]{1,0:T(8,128)(2,1)} %wq_hbm.1), custom_call_target="tpu_custom_call" | custom-call | flops 402653184 | bytes 12582912 | tf_op jit(solution)/shard_map/pallas_call | solution.py:313
  34.0 1.6 %shard_map.69 = (bf16[3,16384]{1,0:T(4,128)(2,1)}, bf16[48,128]{1,0:T(8,128)(2,1)}) custom-call(bf16[3,16384]{1,0:T(4,128)(2,1)} %get-tuple-element.4.hid_in, bf16[48,128]{1,0:T(8,128)(2,1)} %get-tuple-element.5.q_in), custom_call_target="tpu_custom_call" | custom-call | tf_op jit(solution)/shard_map/pallas_call | solution.py:351
